TPU v7x, 512 devices: a whole 4x8x8 slice. The times are simulated.
512 devices in a mesh: seq: 64 (over x, z, core), head: 8 (over y).
Axes of the slice: x: 4, y: 8, z: 8, core: 2. Of those that a mesh axis runs over, the one named last changes fastest.
Arguments:
- queries: bfloat16 [40960, 5120], P(('seq', 'head')), may hold values from -128 to 128
- keys: bfloat16 [40960, 5120], P(('seq', 'head')), may hold values from -128 to 128
- values: bfloat16 [40960, 5120], P(('seq', 'head')), may hold values from -6 to 6
- query_gain: float32 [5120], replicated, may hold values from 1 to 4
- key_gain: float32 [5120], replicated, may hold values from 1 to 4
- level_gate: float32 [30, 5120], replicated, may hold values from -4 to 4
- clip_lengths: int32 [16, 4], replicated, may hold values from 1 to 960, 2560 in all within a row
- levels: int32 [16, 4], replicated, may hold values from 0 to 29, as said below
Outputs:
- gated_output: bfloat16 [40960, 5120], P(('seq', 'head'))
Inputs may be any that keep to these rules, and one draw needn't show every extreme that they name: `clip_lengths`: each row sums to 2560; its largest entry is 960. Along each row the levels never fall; the first is 0, the third is above 0, the last is 29.
All inputs are finite; a program needn't handle non-finite values.
Results may differ from a plain program's by a relative error of at most 0.012.
The roundings to bfloat16 on the way count: a program that leaves them out, or rounds other values in their place, can miss the bound.
Values may be sent and summed in bfloat16 or wider, within the bound.
No kernel may reach another device: no remote copies, remote signals or barrier semaphores. Data moves between devices by JAX's collectives and lax.ppermute only.
A program may use at most 128 MiB of HBM per device.

v0:
```python
import functools
import math

import jax
import jax.numpy as jnp
from jax import lax
from jax.experimental import pallas as pl
from jax.experimental.pallas import tpu as pltpu
from jax.sharding import Mesh
from jax.sharding import PartitionSpec as P

HD = 128
GROUP = 4
CLIPS = 4
PLANE = 32
EXTRA = 8

epsilon = 1e-06
very_negative = -1e30
exponent_scale = math.log2(math.e) / math.sqrt(HD)

VMEM_BYTES = 56 * 1024 * 1024


def vmem():
    return pl.BlockSpec(memory_space=pltpu.VMEM)


def smem():
    return pl.BlockSpec(memory_space=pltpu.SMEM)


def normalize_kernel(q_ref, k_ref, v_ref, qg_ref, kg_ref, own_ref, extra_ref):
    rows, width = q_ref.shape

    def inverse_rms(ref):
        total = jnp.zeros((rows, HD), jnp.float32)
        for head in range(width // HD):
            block = ref[:, head * HD : (head + 1) * HD].astype(jnp.float32)
            total = total + block * block
        mean = jnp.sum(total, axis=1, keepdims=True) / width
        return jnp.broadcast_to(lax.rsqrt(mean + epsilon), (rows, HD))

    inverse_q, inverse_k = inverse_rms(q_ref), inverse_rms(k_ref)
    for head in range(PLANE + EXTRA):
        target, place = (own_ref, head) if head < PLANE else (extra_ref, head - PLANE)
        columns = slice(head * HD, (head + 1) * HD)
        for part, (ref, gain_ref, inverse) in enumerate(
            ((q_ref, qg_ref, inverse_q), (k_ref, kg_ref, inverse_k))
        ):
            block = ref[:, columns].astype(jnp.float32)
            target[place, part] = (block * inverse * gain_ref[:, columns]).astype(jnp.bfloat16)
        target[place, 2] = v_ref[:, columns]


def normalize(queries, keys, values, query_gain, key_gain):
    rows = queries.shape[0]
    return pl.pallas_call(
        normalize_kernel,
        out_shape=[
            jax.ShapeDtypeStruct((PLANE, 3, rows, HD), jnp.bfloat16),
            jax.ShapeDtypeStruct((EXTRA, 3, rows, HD), jnp.bfloat16),
        ],
        in_specs=[vmem()] * 5,
        out_specs=[vmem()] * 2,
        compiler_params=pltpu.CompilerParams(vmem_limit_bytes=VMEM_BYTES),
        cost_estimate=pl.CostEstimate(flops=5_000_000, bytes_accessed=5_000_000, transcendentals=160),
    )(queries, keys, values, query_gain[None, :], key_gain[None, :])


def clip_of(positions, ends):
    result = jnp.zeros_like(positions)
    for boundary in range(CLIPS - 1):
        result = result + (positions >= ends[boundary]).astype(jnp.int32)
    return result


def pick(clip_ids, options):
    result = options[0]
    for clip_id in range(1, CLIPS):
        result = jnp.where(clip_ids == clip_id, options[clip_id], result)
    return result


def clip_table(lengths_ref, levels_ref):
    video = lax.axis_index("v")
    ends, total = [], 0
    for clip_id in range(CLIPS):
        total = total + lengths_ref[video, clip_id]
        ends.append(total)
    return ends, [levels_ref[video, clip_id] for clip_id in range(CLIPS)]


def blocked_columns(positions, ends):
    lanes = lax.broadcasted_iota(jnp.int32, positions.shape, 1)
    later = jnp.logical_and(clip_of(positions, ends) > lanes, lanes < CLIPS)
    return jnp.where(later, very_negative, 0.0).astype(jnp.bfloat16)


def clip_columns(clip_ids):
    lanes = lax.broadcasted_iota(jnp.int32, clip_ids.shape, 1)
    return jnp.where(clip_ids == lanes, 1.0, 0.0).astype(jnp.bfloat16)


def attend(query_block, positions, last, key_ref, value_of, score_ref, chunk, ends, levels, gates, write):
    rows, length = score_ref.shape
    clip_ids = clip_of(positions, ends)
    last_clip = clip_of(last, ends)
    live = pick(last_clip, levels) > 0
    chunks = (pick(last_clip, ends) + chunk - 1) // chunk

    def fold(count, extended):
        peak = jnp.full((rows, HD), very_negative, jnp.float32)
        for step in range(count):
            scores = lax.dot_general(
                extended,
                key_ref[step * chunk : (step + 1) * chunk, :],
                (((1,), (1,)), ((), ())),
                preferred_element_type=jnp.float32,
            )
            score_ref[:, step * chunk : (step + 1) * chunk] = scores
            for part in range(chunk // HD):
                peak = jnp.maximum(peak, scores[:, part * HD : (part + 1) * HD])
        peak = jnp.max(peak, axis=1, keepdims=True) * exponent_scale
        peak = jnp.broadcast_to(peak, (rows, HD))
        total = jnp.zeros((rows, HD), jnp.float32)
        weighted = jnp.zeros((rows, HD), jnp.float32)
        for step in range(count):
            rounded = []
            for part in range(chunk // HD):
                start = step * chunk + part * HD
                weights = jnp.exp2(score_ref[:, start : start + HD] * exponent_scale - peak)
                total = total + weights
                rounded.append(weights.astype(jnp.bfloat16))
            weighted = weighted + jnp.dot(
                jnp.concatenate(rounded, axis=1),
                value_of(step),
                preferred_element_type=jnp.float32,
            )
        attention = weighted / jnp.sum(total, axis=1, keepdims=True)
        attention = attention.astype(jnp.bfloat16).astype(jnp.float32)
        gated = pick(clip_ids, [gates(level) for level in levels]) * attention
        gated = jnp.where(pick(clip_ids, levels) > 0, gated, 0.0)
        write(gated.astype(jnp.bfloat16))

    @pl.when(live)
    def _():
        extended = jnp.concatenate([query_block(), clip_columns(clip_ids)], axis=1)
        for count in range(1, length // chunk + 1):
            pl.when(chunks == count)(functools.partial(fold, count, extended))

    @pl.when(jnp.logical_not(live))
    def _():
        write(jnp.zeros((rows, HD), jnp.bfloat16))


def attention_kernel(
    lengths_ref, levels_ref, gate_ref, query_ref, held_ref, out_ref, key_ref, score_ref, level_ref,
    *, head_of, first_of, places, chunk,
):
    query_place, key_place, value_place = places
    blocks, _, block_rows, _ = query_ref.shape
    rows, length = score_ref.shape
    tile_blocks, chunk_blocks = rows // block_rows, chunk // block_rows
    ends, levels = clip_table(lengths_ref, levels_ref)
    level_ref[...] = gate_ref[:, pl.ds(pl.multiple_of(head_of() * HD, HD), HD)]

    def fill(step, _):
        start = pl.multiple_of(step * chunk, chunk)
        key_ref[pl.ds(start, chunk), 0:HD] = held_ref[
            pl.ds(step * chunk_blocks, chunk_blocks), key_place
        ].reshape(chunk, HD)
        positions = start + lax.broadcasted_iota(jnp.int32, (chunk, HD), 0)
        key_ref[pl.ds(start, chunk), HD : 2 * HD] = blocked_columns(positions, ends)
        return 0

    lax.fori_loop(0, length // chunk, fill, 0)

    def tile(index, _):
        first = first_of() + index * rows
        blocks_here = pl.ds(index * tile_blocks, tile_blocks)

        def write(gated):
            out_ref[blocks_here] = gated.reshape(tile_blocks, block_rows, HD)

        attend(
            lambda: query_ref[blocks_here, query_place].reshape(rows, HD),
            first + lax.broadcasted_iota(jnp.int32, (rows, HD), 0),
            first + rows - 1,
            key_ref,
            lambda step: held_ref[
                step * chunk_blocks : (step + 1) * chunk_blocks, value_place
            ].reshape(chunk, HD),
            score_ref,
            chunk,
            ends,
            levels,
            lambda level: level_ref[pl.ds(level, 1), :],
            write,
        )
        return 0

    lax.fori_loop(0, blocks * block_rows // rows, tile, 0)


def attention(clip_lengths, levels, level_gate, queries, held, head_of, first_of, places, rows=320, chunk=640):
    blocks, _, block_rows, _ = queries.shape
    length = held.shape[0] * block_rows
    work = blocks * block_rows * length
    return pl.pallas_call(
        functools.partial(
            attention_kernel, head_of=head_of, first_of=first_of, places=places, chunk=chunk
        ),
        out_shape=jax.ShapeDtypeStruct((blocks, block_rows, HD), jnp.bfloat16),
        in_specs=[smem(), smem(), vmem(), vmem(), vmem()],
        out_specs=vmem(),
        scratch_shapes=[
            pltpu.VMEM((length, 2 * HD), jnp.bfloat16),
            pltpu.VMEM((rows, length), jnp.float32),
            pltpu.VMEM((level_gate.shape[0], HD), jnp.float32),
        ],
        compiler_params=pltpu.CompilerParams(vmem_limit_bytes=VMEM_BYTES),
        cost_estimate=pl.CostEstimate(
            flops=1200 * work, bytes_accessed=3_000_000, transcendentals=work
        ),
    )(clip_lengths, levels, level_gate, queries, held)


def assemble_kernel(own_ref, extra_ref, out_ref):
    for head in range(PLANE):
        out_ref[:, head * HD : (head + 1) * HD] = own_ref[head]
    for head in range(EXTRA):
        out_ref[:, (PLANE + head) * HD : (PLANE + head + 1) * HD] = extra_ref[head]


def assemble(own, extra):
    rows = own.shape[1]
    return pl.pallas_call(
        assemble_kernel,
        out_shape=jax.ShapeDtypeStruct((rows, (PLANE + EXTRA) * HD), jnp.bfloat16),
        in_specs=[vmem()] * 2,
        out_specs=vmem(),
        compiler_params=pltpu.CompilerParams(vmem_limit_bytes=VMEM_BYTES),
        cost_estimate=pl.CostEstimate(flops=0, bytes_accessed=1_700_000, transcendentals=0),
    )(own, extra)


def local(queries, keys, values, query_gain, key_gain, level_gate, clip_lengths, levels):
    own, extra = normalize(queries, keys, values, query_gain, key_gain)
    extra_held = lax.all_to_all(extra, "y", 0, 0, tiled=True)
    own_held = lax.all_to_all(own, ("x", "y"), 0, 0, tiled=True)
    gathered = lax.all_gather(extra_held[:, 1:], "x", axis=0, tiled=True)
    table = (clip_lengths, levels, level_gate)
    extra_out = attention(
        *table,
        extra_held,
        gathered,
        head_of=lambda: PLANE + lax.axis_index("y"),
        first_of=lambda: lax.axis_index("x") * 640,
        places=(0, 0, 1),
    )
    extra_back = lax.all_to_all(extra_out, "y", 0, 0, tiled=True)
    own_out = attention(
        *table,
        own_held,
        own_held,
        head_of=lambda: lax.axis_index("x") * 8 + lax.axis_index("y"),
        first_of=lambda: 0,
        places=(0, 1, 2),
    )
    own_back = lax.all_to_all(own_out, ("x", "y"), 0, 0, tiled=True)
    return assemble(own_back, extra_back)


def solution(mesh):
    videos = mesh.shape["seq"] // GROUP
    finer = Mesh(mesh.devices.reshape(GROUP, videos, EXTRA), ("x", "v", "y"))
    rows = P(("x", "v", "y"), None)
    return jax.shard_map(
        local,
        mesh=finer,
        in_specs=(rows, rows, rows, P(), P(), P(), P(), P()),
        out_specs=rows,
        check_vma=False,
    )
```

profile of v0, /device:TPU:128, one launch (start us, length us, event | category | flops | bytes accessed | tf_op | source)
XLA Modules:
  0.0 152.4 jit_solution(11195977336679272162)
XLA Ops:
  6.5 3.7 %shard_map.82 = (bf16[32,3,80,128]{3,2,1,0:T(8,128)(2,1)}, bf16[8,3,80,128]{3,2,1,0:T(8,128)(2,1)}) custom-call(bf16[80,5120]{1,0:T(8,128)(2,1)} %q_ref.1, bf16[80,5120]{1,0:T(8,128)(2,1)} %k_ref.1, bf16[80,5120]{1,0:T(8,128)(2,1)} %v_ref.1, f32[1,5120]{1,0:T(1,128)} %bitcast.2, f32[1,5120]{1,0:T(1,128)} %bitcast.3), custom_call_target="tpu_custom_call" | custom-call | flops 5000000 | bytes 5000000 | tf_op jit(solution)/shard_map/pallas_call | solution.py:58
  10.3 23.9 %all_to_all.20.query_ref = bf16[8,3,80,128]{3,2,1,0:T(8,128)(2,1)S(1)} all-to-all(bf16[8,3,80,128]{3,2,1,0:T(8,128)(2,1)} %get-tuple-element.8), channel_id=1, replica_groups=mesh['x'=4,'v'=16,'y'=8] {'y'}, dimensions={0} | all-to-all | bytes 983040 | tf_op jit(solution)/shard_map/all_to_all | solution.py:250
  34.2 0.0 copy-start.1
  34.2 0.0 copy-start.3
  34.2 0.0 copy-start.4
  34.2 4.8 %all-to-all-start = ((bf16[32,3,80,128]{3,2,1,0:T(8,128)(2,1)}), bf16[32,3,80,128]{3,2,1,0:T(8,128)(2,1)S(1)}, u32[]{:S(2)}, u32[]{:S(2)}) async-start(bf16[32,3,80,128]{3,2,1,0:T(8,128)(2,1)} %get-tuple-element.7), calls=%async_computation | async-start | bytes 3932160 | tf_op jit(solution)/shard_map/all_to_all | solution.py:251
  39.0 0.0 all-gather.2.cloned.1.call-start
  39.0 0.0 copy-done.1
  39.0 0.8 slice.4
  39.8 0.0 all-gather.2.cloned.1.call-update
  39.8 0.0 copy-done.3
  39.8 0.7 copy.13.lengths_ref
  40.5 0.0 copy-done.4
  40.5 0.7 copy.14.levels_ref
  41.2 43.0 %all-gather.2.cloned.1.call-done.held_ref = bf16[32,2,80,128]{3,2,1,0:T(8,128)(2,1)} async-done(((bf16[8,2,80,128]{3,2,1,0:T(8,128)(2,1)}), bf16[32,2,80,128]{3,2,1,0:T(8,128)(2,1)}) %all-gather.2.cloned.1.call-update) | async-done | bytes 1310736 | tf_op jit(solution)/shard_map/all_gather | solution.py:252
  84.2 4.6 %shard_map.84 = bf16[8,80,128]{2,1,0:T(8,128)(2,1)} custom-call(s32[16,4]{1,0:T(8,128)} %copy.13.lengths_ref, s32[16,4]{1,0:T(8,128)} %copy.14.levels_ref, f32[30,5120]{1,0:T(8,128)} %gate_ref.3, bf16[8,3,80,128]{3,2,1,0:T(8,128)(2,1)} %copy-done.1, bf16[32,2,80,128]{3,2,1,0:T(8,128)(2,1)} %all-gather.2.cloned.1.call-done.held_ref), custom_call_target="tpu_custom_call" | custom-call | flops 1966080000 | bytes 3000000 | tf_op jit(solution)/shard_map/pallas_call | solution.py:210
  88.8 0.0 all-to-all-done.query_ref.held_ref
  88.8 0.0 copy-start
  88.8 7.1 %all-to-all-start.3 = ((bf16[8,80,128]{2,1,0:T(8,128)(2,1)}), bf16[8,80,128]{2,1,0:T(8,128)(2,1)S(1)}, u32[]{:S(2)}, u32[]{:S(2)}) async-start(bf16[8,80,128]{2,1,0:T(8,128)(2,1)} %shard_map.84), calls=%async_computation.3 | async-start | bytes 327680 | tf_op jit(solution)/shard_map/all_to_all | solution.py:262
  95.9 0.0 copy-done
  95.9 15.6 %shard_map.83 = bf16[32,80,128]{2,1,0:T(8,128)(2,1)} custom-call(s32[16,4]{1,0:T(8,128)} %copy.13.lengths_ref, s32[16,4]{1,0:T(8,128)} %copy.14.levels_ref, f32[30,5120]{1,0:T(8,128)} %gate_ref.3, bf16[32,3,80,128]{3,2,1,0:T(8,128)(2,1)} %copy-done, bf16[32,3,80,128]{3,2,1,0:T(8,128)(2,1)} %copy-done), custom_call_target="tpu_custom_call" | custom-call | flops 7864320000 | bytes 3000000 | tf_op jit(solution)/shard_map/pallas_call | solution.py:210
  111.5 0.0 all-to-all-done.3.extra_ref
  111.5 0.0 copy-start.2
  111.5 31.8 %all_to_all.21.own_ref = bf16[32,80,128]{2,1,0:T(8,128)(2,1)} all-to-all(bf16[32,80,128]{2,1,0:T(8,128)(2,1)} %shard_map.83), channel_id=1, replica_groups=mesh['x'=4,'v'=16,'y'=8] {'x','y'}, dimensions={0} | all-to-all | bytes 1310720 | tf_op jit(solution)/shard_map/all_to_all | solution.py:271
  143.3 0.0 copy-done.2
  143.3 2.2 %shard_map.85 = bf16[80,5120]{1,0:T(8,128)(2,1)} custom-call(bf16[32,80,128]{2,1,0:T(8,128)(2,1)} %all_to_all.21.own_ref, bf16[8,80,128]{2,1,0:T(8,128)(2,1)} %copy-done.2), custom_call_target="tpu_custom_call" | custom-call | bytes 1700000 | tf_op jit(solution)/shard_map/pallas_call | solution.py:238
Async XLA Ops:
  34.2 4.9 %copy-start.1 = (bf16[8,3,80,128]{3,2,1,0:T(8,128)(2,1)}, bf16[8,3,80,128]{3,2,1,0:T(8,128)(2,1)S(1)}, u32[]{:S(2)}) copy-start(bf16[8,3,80,128]{3,2,1,0:T(8,128)(2,1)S(1)} %all_to_all.20.query_ref) | copy-start | bytes 1474564
  34.2 5.7 %copy-start.3 = (s32[16,4]{0,1:T(4,128)S(1)}, s32[16,4]{0,1:T(4,128)}, u32[]{:S(2)}) copy-start(s32[16,4]{0,1:T(4,128)} %param.14) | copy-start | bytes 772
  34.2 6.4 %copy-start.4 = (s32[16,4]{0,1:T(4,128)S(1)}, s32[16,4]{0,1:T(4,128)}, u32[]{:S(2)}) copy-start(s32[16,4]{0,1:T(4,128)} %param.15) | copy-start | bytes 772
  34.2 54.6 %all-to-all-start = ((bf16[32,3,80,128]{3,2,1,0:T(8,128)(2,1)}), bf16[32,3,80,128]{3,2,1,0:T(8,128)(2,1)S(1)}, u32[]{:S(2)}, u32[]{:S(2)}) async-start(bf16[32,3,80,128]{3,2,1,0:T(8,128)(2,1)} %get-tuple-element.7), calls=%async_computation | async-start | bytes 3932160 | tf_op jit(solution)/shard_map/all_to_all | solution.py:251
  39.0 45.2 %all-gather.2.cloned.1.call-start = ((), (), s32[]{:S(2)}) async-start(), calls=%async_computation.4 | async-start | bytes 1638400 | tf_op jit(solution)/shard_map/all_gather | solution.py:252
  88.8 7.1 %copy-start = (bf16[32,3,80,128]{3,2,1,0:T(8,128)(2,1)}, bf16[32,3,80,128]{3,2,1,0:T(8,128)(2,1)S(1)}, u32[]{:S(2)}) copy-start(bf16[32,3,80,128]{3,2,1,0:T(8,128)(2,1)S(1)} %all-to-all-done.query_ref.held_ref) | copy-start | bytes 5898244
  88.8 22.8 %all-to-all-start.3 = ((bf16[8,80,128]{2,1,0:T(8,128)(2,1)}), bf16[8,80,128]{2,1,0:T(8,128)(2,1)S(1)}, u32[]{:S(2)}, u32[]{:S(2)}) async-start(bf16[8,80,128]{2,1,0:T(8,128)(2,1)} %shard_map.84), calls=%async_computation.3 | async-start | bytes 327680 | tf_op jit(solution)/shard_map/all_to_all | solution.py:262
  111.5 31.8 %copy-start.2 = (bf16[8,80,128]{2,1,0:T(8,128)(2,1)}, bf16[8,80,128]{2,1,0:T(8,128)(2,1)S(1)}, u32[]{:S(2)}) copy-start(bf16[8,80,128]{2,1,0:T(8,128)(2,1)S(1)} %all-to-all-done.3.extra_ref) | copy-start | bytes 491524
Sparse Core Ops, SparseCore 0:
  41.9 42.1 all-gather.1
where the time goes:
time: 153 us; the launch traced here: 152 us
  blocking collectives  55.7 us (36%)
  waiting for transfers between devices  43 us (28%)
  Pallas kernels  26.1 us (17%)
  between operations  13.4 us (9%)
  starting transfers between devices  12 us (8%)
  local copies, waits for them, and re-layouts  2.13 us (1%)
    all_gather x1, waiting for transfers between devices, local(): gathered = lax.all_gather(extra_held[:, 1:], 'x', axis=0, tiled=True)  43 us
    all_to_all x1, blocking collectives, local(): own_back = lax.all_to_all(own_out, ('x', 'y'), 0, 0, tiled=True)  31.8 us
    all_to_all x1, blocking collectives, local(): extra_held = lax.all_to_all(extra, 'y', 0, 0, tiled=True)  23.9 us
    pallas_call x2, Pallas kernels, attention(): pl.pallas_call(functools.partial(attention_kernel, head_of=head_of, first...  20.2 us
    all_to_all x1, starting transfers between devices, local(): extra_back = lax.all_to_all(extra_out, 'y', 0, 0, tiled=True)  7.14 us
    all_to_all x1, starting transfers between devices, local(): own_held = lax.all_to_all(own, ('x', 'y'), 0, 0, tiled=True)  4.82 us
    pallas_call x1, Pallas kernels, normalize(): pl.pallas_call(normalize_kernel, out_shape=[jax.ShapeDtypeStruct((PLANE,...  3.73 us
  transfers between devices with their start and end apart: 3, of which 1 were waited for; matrix products, arithmetic and copies ran while one was open for 1% of the time, Pallas kernels for 13%

commit v1 on v0

v1 whole, which is shorter than its diff:
```python
import functools
import math

import jax
import jax.numpy as jnp
from jax import lax
from jax.experimental import pallas as pl
from jax.experimental.pallas import tpu as pltpu
from jax.sharding import Mesh
from jax.sharding import PartitionSpec as P

HD = 128
GROUP = 4
CLIPS = 4
PLANE = 32
EXTRA = 8

epsilon = 1e-06
very_negative = -1e30
exponent_scale = math.log2(math.e) / math.sqrt(HD)

VMEM_BYTES = 24 * 1024 * 1024
LARGE_VMEM = 56 * 1024 * 1024
SMALL_VMEM = 12 * 1024 * 1024


def vmem():
    return pl.BlockSpec(memory_space=pltpu.VMEM)


def smem():
    return pl.BlockSpec(memory_space=pltpu.SMEM)


def inverse_rms(ref):
    rows, width = ref.shape
    total = jnp.zeros((rows, HD), jnp.float32)
    for head in range(width // HD):
        block = ref[:, head * HD : (head + 1) * HD].astype(jnp.float32)
        total = total + block * block
    mean = jnp.sum(total, axis=1, keepdims=True) / width
    return jnp.broadcast_to(lax.rsqrt(mean + epsilon), (rows, HD))


def lay_out(q_ref, k_ref, v_ref, qg_ref, kg_ref, inverses, out_ref):
    for head in range(out_ref.shape[0]):
        columns = slice(head * HD, (head + 1) * HD)
        for part, (ref, gain_ref, inverse) in enumerate(
            ((q_ref, qg_ref, inverses[0]), (k_ref, kg_ref, inverses[1]))
        ):
            block = ref[:, columns].astype(jnp.float32)
            out_ref[head, part] = (block * inverse * gain_ref[:, columns]).astype(jnp.bfloat16)
        out_ref[head, 2] = v_ref[:, columns]


def extra_norm_kernel(q_ref, k_ref, v_ref, qg_ref, kg_ref, out_ref, inverse_ref):
    inverses = [inverse_rms(q_ref), inverse_rms(k_ref)]
    inverse_ref[0], inverse_ref[1] = inverses
    columns = slice(PLANE * HD, (PLANE + EXTRA) * HD)
    lay_out(q_ref.at[:, columns], k_ref.at[:, columns], v_ref, qg_ref, kg_ref, inverses, out_ref)


def own_norm_kernel(q_ref, k_ref, v_ref, qg_ref, kg_ref, inverse_ref, out_ref):
    inverses = [inverse_ref[0], inverse_ref[1]]
    lay_out(q_ref, k_ref, v_ref, qg_ref, kg_ref, inverses, out_ref)


def normalize(queries, keys, values, query_gain, key_gain):
    rows, width = queries.shape
    own_width, extra_width = PLANE * HD, EXTRA * HD

    def block(height, count, place=0):
        return pl.BlockSpec((height, count), lambda step: (0, place))

    def full(*shape):
        return pl.BlockSpec(shape, lambda step: (0,) * len(shape))

    whole = (queries, keys, values, query_gain[None, :], key_gain[None, :])
    params = pltpu.CompilerParams(vmem_limit_bytes=LARGE_VMEM)
    last = own_width // extra_width
    extra, inverses = pl.pallas_call(
        extra_norm_kernel,
        grid=(1,),
        out_shape=[
            jax.ShapeDtypeStruct((EXTRA, 3, rows, HD), jnp.bfloat16),
            jax.ShapeDtypeStruct((2, rows, HD), jnp.float32),
        ],
        in_specs=[block(rows, width)] * 2
        + [block(rows, extra_width, last)]
        + [block(1, extra_width, last)] * 2,
        out_specs=[full(EXTRA, 3, rows, HD), full(2, rows, HD)],
        compiler_params=params,
        cost_estimate=pl.CostEstimate(flops=3_000_000, bytes_accessed=3_000_000, transcendentals=160),
    )(*whole)
    own = pl.pallas_call(
        own_norm_kernel,
        grid=(1,),
        out_shape=jax.ShapeDtypeStruct((PLANE, 3, rows, HD), jnp.bfloat16),
        in_specs=[block(rows, own_width)] * 3 + [block(1, own_width)] * 2 + [full(2, rows, HD)],
        out_specs=full(PLANE, 3, rows, HD),
        compiler_params=params,
        cost_estimate=pl.CostEstimate(flops=3_000_000, bytes_accessed=5_000_000, transcendentals=0),
    )(*whole, inverses)
    return own, extra


def clip_of(positions, ends):
    result = jnp.zeros_like(positions)
    for boundary in range(CLIPS - 1):
        result = result + (positions >= ends[boundary]).astype(jnp.int32)
    return result


def pick(clip_ids, options):
    result = options[0]
    for clip_id in range(1, CLIPS):
        result = jnp.where(clip_ids == clip_id, options[clip_id], result)
    return result


def clip_table(lengths_ref, levels_ref):
    video = lax.axis_index("v")
    ends, total = [], 0
    for clip_id in range(CLIPS):
        total = total + lengths_ref[clip_id, video]
        ends.append(total)
    return ends, [levels_ref[clip_id, video] for clip_id in range(CLIPS)]


def blocked_rows(start, count, ends):
    clip_ids = clip_of(start + lax.broadcasted_iota(jnp.int32, (16, count), 1), ends)
    rows = lax.broadcasted_iota(jnp.int32, (16, count), 0)
    later = jnp.logical_and(clip_ids > rows, rows < CLIPS)
    return jnp.where(later, very_negative, 0.0).astype(jnp.bfloat16)


def clip_columns(clip_ids):
    lanes = lax.broadcasted_iota(jnp.int32, clip_ids.shape, 1)
    return jnp.where(clip_ids == lanes, 1.0, 0.0).astype(jnp.bfloat16)


def attention_kernel(
    lengths_ref, levels_ref, gate_ref, query_ref, *refs, piece_count, first_of, places, chunk
):
    piece_refs, (out_ref, key_ref, value_ref, score_ref) = refs[:piece_count], refs[piece_count:]
    query_place, key_place, value_place = places
    blocks, _, block_rows, _ = query_ref.shape
    rows, _ = score_ref.shape
    tile_blocks, chunk_blocks = rows // block_rows, chunk // block_rows
    tiles = blocks // tile_blocks
    ends, levels = clip_table(lengths_ref, levels_ref)

    length, piece_rows = key_ref.shape[1], key_ref.shape[1] // piece_count
    for turn, piece_ref in enumerate(piece_refs):
        place = (lax.axis_index("x") + GROUP - turn) % GROUP if piece_count > 1 else 0
        for step in range(piece_rows // chunk):
            start = place * piece_rows + step * chunk
            where = pl.ds(pl.multiple_of(start, chunk), chunk)
            source = slice(step * chunk_blocks, (step + 1) * chunk_blocks)
            key_ref[0:HD, where] = piece_ref[source, key_place].reshape(chunk, HD).T
            key_ref[HD : HD + 16, where] = blocked_rows(start, chunk, ends)
            if piece_count > 1:
                value_ref[where, :] = piece_ref[source, value_place].reshape(chunk, HD)
    key_ref[HD + 16 :, :] = jnp.zeros((HD - 16, length), jnp.bfloat16)

    def values_of(step):
        if piece_count > 1:
            return value_ref[step * chunk : (step + 1) * chunk, :]
        return piece_refs[0][step * chunk_blocks : (step + 1) * chunk_blocks, value_place].reshape(chunk, HD)

    def first_row(tile):
        return first_of() + tile * rows

    def last_clip(tile):
        return clip_of(first_row(tile) + rows - 1, ends)

    def chunk_count(tile):
        return (pick(last_clip(tile), ends) + chunk - 1) // chunk

    def clips_of_rows(tile):
        return clip_of(first_row(tile) + lax.broadcasted_iota(jnp.int32, (rows, HD), 0), ends)

    def blocks_of(tile):
        return pl.ds(tile * tile_blocks, tile_blocks)

    def queries_of(tile):
        held = query_ref[blocks_of(tile), query_place].reshape(rows, HD)
        return jnp.concatenate([held, clip_columns(clips_of_rows(tile))], axis=1)

    def whole(tile, count):
        extended = queries_of(tile)
        peak = jnp.full((rows, HD), very_negative, jnp.float32)
        for step in range(count):
            here = slice(step * chunk, (step + 1) * chunk)
            scores = jnp.dot(extended, key_ref[:, here], preferred_element_type=jnp.float32)
            score_ref[:, here] = scores
            for part in range(chunk // HD):
                peak = jnp.maximum(peak, scores[:, part * HD : (part + 1) * HD])
        peak = jnp.max(peak, axis=1, keepdims=True) * exponent_scale
        peak = jnp.broadcast_to(peak, (rows, HD))
        total = jnp.zeros((rows, HD), jnp.float32)
        weighted = jnp.zeros((rows, HD), jnp.float32)
        for step in range(count):
            rounded = []
            for part in range(chunk // HD):
                start = step * chunk + part * HD
                weights = jnp.exp2(score_ref[:, start : start + HD] * exponent_scale - peak)
                total = total + weights
                rounded.append(weights.astype(jnp.bfloat16))
            weighted = weighted + jnp.dot(
                jnp.concatenate(rounded, axis=1), values_of(step), preferred_element_type=jnp.float32
            )
        attention = weighted / jnp.sum(total, axis=1, keepdims=True)
        attention = attention.astype(jnp.bfloat16).astype(jnp.float32)
        positions = first_row(tile) + lax.broadcasted_iota(jnp.int32, (rows, HD), 0)
        gate = gates[0]
        for clip_id in range(1, CLIPS):
            gate = jnp.where(positions >= ends[clip_id - 1], gates[clip_id], gate)
        gated = (gate * attention).astype(jnp.bfloat16)
        out_ref[blocks_of(tile)] = gated.reshape(tile_blocks, block_rows, HD)

    gates = [
        jnp.where(level > 0, gate_ref[pl.ds(level, 1), :], 0.0) for level in levels
    ]
    skipped = 0
    for tile in range(tiles):
        skipped = skipped + (pick(last_clip(tile), levels) <= 0).astype(jnp.int32)

    def clear(tile, _):
        out_ref[blocks_of(tile)] = jnp.zeros((tile_blocks, block_rows, HD), jnp.bfloat16)
        return 0

    def one(tile, _):
        needed = chunk_count(tile)
        for count in range(1, length // chunk + 1):
            pl.when(needed == count)(functools.partial(whole, tile, count))
        return 0

    lax.fori_loop(0, skipped, clear, 0)
    lax.fori_loop(skipped, tiles, one, 0)


def attention(
    clip_lengths, levels, level_gate, queries, pieces, first_of, places, rows=320, chunk=640
):
    blocks, _, block_rows, _ = queries.shape
    length = sum(piece.shape[0] for piece in pieces) * block_rows
    work = blocks * block_rows * length
    scores = pltpu.VMEM((rows, length), jnp.float32)
    return pl.pallas_call(
        functools.partial(
            attention_kernel,
            piece_count=len(pieces),
            first_of=first_of,
            places=places,
            chunk=chunk,
        ),
        out_shape=jax.ShapeDtypeStruct((blocks, block_rows, HD), jnp.bfloat16),
        in_specs=[smem(), smem()] + [vmem()] * (2 + len(pieces)),
        out_specs=vmem(),
        scratch_shapes=[
            pltpu.VMEM((2 * HD, length), jnp.bfloat16),
            pltpu.VMEM((length, HD), jnp.bfloat16),
            scores,
        ],
        compiler_params=pltpu.CompilerParams(vmem_limit_bytes=VMEM_BYTES),
        cost_estimate=pl.CostEstimate(
            flops=1200 * work, bytes_accessed=3_000_000, transcendentals=work
        ),
    )(clip_lengths, levels, level_gate, queries, *pieces)


def assemble_kernel(own_ref, extra_ref, out_ref):
    for head in range(PLANE):
        out_ref[:, head * HD : (head + 1) * HD] = own_ref[head]
    for head in range(EXTRA):
        out_ref[:, (PLANE + head) * HD : (PLANE + head + 1) * HD] = extra_ref[head]


def assemble(own, extra):
    rows = own.shape[1]
    return pl.pallas_call(
        assemble_kernel,
        out_shape=jax.ShapeDtypeStruct((rows, (PLANE + EXTRA) * HD), jnp.bfloat16),
        in_specs=[vmem()] * 2,
        out_specs=vmem(),
        compiler_params=pltpu.CompilerParams(vmem_limit_bytes=SMALL_VMEM),
        cost_estimate=pl.CostEstimate(flops=0, bytes_accessed=1_700_000, transcendentals=0),
    )(own, extra)


def along_x(value, steps):
    pairs = [(source, (source + steps) % GROUP) for source in range(GROUP)]
    return lax.ppermute(value, "x", pairs)


def local(queries, keys, values, query_gain, key_gain, level_gate, clip_lengths, levels):
    own, extra = normalize(queries, keys, values, query_gain, key_gain)
    extra_held = lax.all_to_all(extra, "y", 0, 0, tiled=True)
    own_held = lax.all_to_all(own, ("x", "y"), 0, 0, tiled=True)
    pieces = [extra_held[:, 1:]]
    pieces += [along_x(pieces[0], steps) for steps in range(1, GROUP)]
    table = (clip_lengths.T, levels.T)
    row, column = lax.axis_index("x"), lax.axis_index("y")
    own_gate = lax.dynamic_slice_in_dim(level_gate, (row * EXTRA + column) * HD, HD, 1)
    extra_gate = lax.dynamic_slice_in_dim(level_gate, (PLANE + column) * HD, HD, 1)
    extra_out = attention(
        *table,
        extra_gate,
        extra_held,
        pieces,
        first_of=lambda: lax.axis_index("x") * 640,
        places=(0, 0, 1),
    )
    extra_back = lax.all_to_all(extra_out, "y", 0, 0, tiled=True)
    own_out = attention(
        *table,
        own_gate,
        own_held,
        [own_held],
        first_of=lambda: 0,
        places=(0, 1, 2),
    )
    own_back = lax.all_to_all(own_out, ("x", "y"), 0, 0, tiled=True)
    return assemble(own_back, extra_back)


def solution(mesh):
    videos = mesh.shape["seq"] // GROUP
    finer = Mesh(mesh.devices.reshape(GROUP, videos, EXTRA), ("x", "v", "y"))
    rows = P(("x", "v", "y"), None)
    return jax.shard_map(
        local,
        mesh=finer,
        in_specs=(rows, rows, rows, P(), P(), P(), P(), P()),
        out_specs=rows,
        check_vma=False,
    )
```

time: 153 us -> 125 us (0.82)
  the two profiles are of different devices: /device:TPU:128 before, /device:TPU:73 now
where the time goes in v1:
time: 125 us
  waiting for transfers between devices  42.4 us (34%)
  blocking collectives  29.2 us (23%)
  starting transfers between devices  29 us (23%)
  Pallas kernels  23.1 us (18%)
    all_to_all x1, blocking collectives, local(): own_back = lax.all_to_all(own_out, ('x', 'y'), 0, 0, tiled=True)  29.2 us
    ppermute x3, waiting for transfers between devices, along_x(): return lax.ppermute(value, 'x', pairs)  26.2 us
    pallas_call x2, Pallas kernels, attention(): pl.pallas_call(functools.partial(attention_kernel, piece_count=len(pieces...  16.3 us
    all_to_all x1, waiting for transfers between devices, local(): extra_held = lax.all_to_all(extra, 'y', 0, 0, tiled=True)  9.52 us
    ppermute x3, starting transfers between devices, along_x(): return lax.ppermute(value, 'x', pairs)  9.28 us
    all_to_all x1, starting transfers between devices, local(): own_held = lax.all_to_all(own, ('x', 'y'), 0, 0, tiled=True)  8.79 us
    all_to_all x1, starting transfers between devices, local(): extra_held = lax.all_to_all(extra, 'y', 0, 0, tiled=True)  6.99 us
    all_to_all x1, waiting for transfers between devices, local(): own_held = lax.all_to_all(own, ('x', 'y'), 0, 0, tiled=True)  6.69 us
  transfers between devices with their start and end apart: 6, of which 5 were waited for; matrix products, arithmetic and copies ran while one was open for 1% of the time, Pallas kernels for 16%

profile of v1, /device:TPU:73, one launch (start us, length us, event | category | flops | bytes accessed | tf_op | source)
XLA Modules:
  0.0 124.5 jit_solution(13584964100231382127)
XLA Ops:
  0.0 2.6 %shard_map.82 = (bf16[8,3,80,128]{3,2,1,0:T(8,128)(2,1)}, f32[2,80,128]{2,1,0:T(8,128)}) custom-call(bf16[80,5120]{1,0:T(8,128)(2,1)} %q_ref.3, bf16[80,5120]{1,0:T(8,128)(2,1)} %k_ref.3, bf16[80,5120]{1,0:T(8,128)(2,1)} %v_ref.3, f32[1,5120]{1,0:T(1,128)} %bitcast.8, f32[1,5120]{1,0:T(1,128)} %bitcast.10), custom_call_target="tpu_custom_call" | custom-call | flops 3000000 | bytes 3000000 | tf_op jit(solution)/shard_map/pallas_call | solution.py:81
  2.7 7.0 %all-to-all-start.2 = ((bf16[8,3,80,128]{3,2,1,0:T(8,128)(2,1)}), bf16[8,3,80,128]{3,2,1,0:T(8,128)(2,1)S(1)}, u32[]{:S(2)}, u32[]{:S(2)}) async-start(bf16[8,3,80,128]{3,2,1,0:T(8,128)(2,1)} %get-tuple-element.8), calls=%async_computation.2 | async-start | bytes 983040 | tf_op jit(solution)/shard_map/all_to_all | solution.py:299
  9.6 3.1 %shard_map.83 = bf16[32,3,80,128]{3,2,1,0:T(8,128)(2,1)} custom-call(bf16[80,5120]{1,0:T(8,128)(2,1)} %q_ref.3, bf16[80,5120]{1,0:T(8,128)(2,1)} %k_ref.3, bf16[80,5120]{1,0:T(8,128)(2,1)} %v_ref.3, f32[1,5120]{1,0:T(1,128)} %bitcast.9, f32[1,5120]{1,0:T(1,128)} %bitcast.11, f32[2,80,128]{2,1,0:T(8,128)} %get-tuple-element.7.inverse_ref), custom_call_target="tpu_custom_call" | custom-call | flops 3000000 | bytes 5000000 | tf_op jit(solution)/shard_map/pallas_call | solution.py:95
  12.8 0.0 copy-start
  12.8 0.0 copy-start.1
  12.8 9.5 %all-to-all-done.2.query_ref = bf16[8,3,80,128]{3,2,1,0:T(8,128)(2,1)S(1)} async-done(((bf16[8,3,80,128]{3,2,1,0:T(8,128)(2,1)}), bf16[8,3,80,128]{3,2,1,0:T(8,128)(2,1)S(1)}, u32[]{:S(2)}, u32[]{:S(2)}) %all-to-all-start.2) | async-done | bytes 491552 | tf_op jit(solution)/shard_map/all_to_all | solution.py:299
  22.3 8.8 %all-to-all-start = ((bf16[32,3,80,128]{3,2,1,0:T(8,128)(2,1)}), bf16[32,3,80,128]{3,2,1,0:T(8,128)(2,1)S(1)}, u32[]{:S(2)}, u32[]{:S(2)}) async-start(bf16[32,3,80,128]{3,2,1,0:T(8,128)(2,1)} %shard_map.83), calls=%async_computation | async-start | bytes 3932160 | tf_op jit(solution)/shard_map/all_to_all | solution.py:300
  31.1 4.4 %collective-permute-start.2 = (bf16[8,2,80,128]{3,2,1,0:T(8,128)(2,1)S(1)}, bf16[8,2,80,128]{3,2,1,0:T(8,128)(2,1)S(1)}, u32[]{:S(2)}, u32[]{:S(2)}) collective-permute-start(bf16[8,2,80,128]{3,2,1,0:T(8,128)(2,1)S(1)} %slice.4.refs_0_), channel_id=1, source_target_pairs={{0,384},{128,0},{256,128},{384,256},{1,385},{129,1},{257,129},{385... | collective-permute-start | bytes 983048 | tf_op jit(solution)/shard_map/ppermute | solution.py:294
  35.5 2.4 %collective-permute-start.1 = (bf16[8,2,80,128]{3,2,1,0:T(8,128)(2,1)S(1)}, bf16[8,2,80,128]{3,2,1,0:T(8,128)(2,1)S(1)}, u32[]{:S(2)}, u32[]{:S(2)}) collective-permute-start(bf16[8,2,80,128]{3,2,1,0:T(8,128)(2,1)S(1)} %slice.4.refs_0_), channel_id=1, source_target_pairs={{0,256},{128,384},{256,0},{384,128},{1,257},{129,385},{257,1},{385... | collective-permute-start | bytes 983048 | tf_op jit(solution)/shard_map/ppermute | solution.py:294
  37.9 2.5 %collective-permute-start = (bf16[8,2,80,128]{3,2,1,0:T(8,128)(2,1)S(1)}, bf16[8,2,80,128]{3,2,1,0:T(8,128)(2,1)}, u32[]{:S(2)}, u32[]{:S(2)}) collective-permute-start(bf16[8,2,80,128]{3,2,1,0:T(8,128)(2,1)S(1)} %slice.4.refs_0_), channel_id=1, source_target_pairs={{0,128},{128,256},{256,384},{384,0},{1,129},{129,257},{257,385},{3... | collective-permute-start | bytes 983048 | tf_op jit(solution)/shard_map/ppermute | solution.py:294
  40.4 0.7 constant_dynamic-slice_fusion
  41.2 7.7 %collective-permute-done.2.refs_3_ = bf16[8,2,80,128]{3,2,1,0:T(8,128)(2,1)S(1)} collective-permute-done((bf16[8,2,80,128]{3,2,1,0:T(8,128)(2,1)S(1)}, bf16[8,2,80,128]{3,2,1,0:T(8,128)(2,1)S(1)}, u32[]{:S(2)}, u32[]{:S(2)}) %collective-permute-start.2) | collective-permute-done | bytes 327712 | tf_op jit(solution)/shard_map/ppermute | solution.py:294
  48.9 2.2 %collective-permute-done.1.refs_2_ = bf16[8,2,80,128]{3,2,1,0:T(8,128)(2,1)S(1)} collective-permute-done((bf16[8,2,80,128]{3,2,1,0:T(8,128)(2,1)S(1)}, bf16[8,2,80,128]{3,2,1,0:T(8,128)(2,1)S(1)}, u32[]{:S(2)}, u32[]{:S(2)}) %collective-permute-start.1) | collective-permute-done | bytes 327712 | tf_op jit(solution)/shard_map/ppermute | solution.py:294
  51.1 16.3 %collective-permute-done.refs_1_ = bf16[8,2,80,128]{3,2,1,0:T(8,128)(2,1)} collective-permute-done((bf16[8,2,80,128]{3,2,1,0:T(8,128)(2,1)S(1)}, bf16[8,2,80,128]{3,2,1,0:T(8,128)(2,1)}, u32[]{:S(2)}, u32[]{:S(2)}) %collective-permute-start) | collective-permute-done | bytes 327712 | tf_op jit(solution)/shard_map/ppermute | solution.py:294
  67.3 0.0 copy-done
  67.3 0.0 copy-done.1
  67.3 4.0 %shard_map.85 = bf16[8,80,128]{2,1,0:T(8,128)(2,1)} custom-call(s32[4,16]{1,0:T(4,128)S(1)} %bitcast.4, s32[4,16]{1,0:T(4,128)S(1)} %bitcast.6, f32[30,128]{1,0:T(8,128)S(1)} %get-tuple-element.9.gate_ref, bf16[8,3,80,128]{3,2,1,0:T(8,128)(2,1)S(1)} %all-to-all-done.2.query_ref, bf16[8,2,80,128]{3,2,1,0:T(8,128)(2,1)S(1)} %slice.4.refs_0_, ...), custom_call_target="tpu_custom_call" | custom-call | flops 1966080000 | bytes 3000000 | tf_op jit(solution)/shard_map/pallas_call | solution.py:250
  71.3 6.7 %all-to-all-done.query_ref.refs_0_ = bf16[32,3,80,128]{3,2,1,0:T(8,128)(2,1)S(1)} async-done(((bf16[32,3,80,128]{3,2,1,0:T(8,128)(2,1)}), bf16[32,3,80,128]{3,2,1,0:T(8,128)(2,1)S(1)}, u32[]{:S(2)}, u32[]{:S(2)}) %all-to-all-start) | async-done | bytes 1966112 | tf_op jit(solution)/shard_map/all_to_all | solution.py:300
  78.0 3.9 %all-to-all-start.3 = ((bf16[8,80,128]{2,1,0:T(8,128)(2,1)}), bf16[8,80,128]{2,1,0:T(8,128)(2,1)S(1)}, u32[]{:S(2)}, u32[]{:S(2)}) async-start(bf16[8,80,128]{2,1,0:T(8,128)(2,1)} %shard_map.85), calls=%async_computation.3 | async-start | bytes 327680 | tf_op jit(solution)/shard_map/all_to_all | solution.py:315
  81.9 12.3 %shard_map.84 = bf16[32,80,128]{2,1,0:T(8,128)(2,1)S(1)} custom-call(s32[4,16]{1,0:T(4,128)S(1)} %bitcast.5, s32[4,16]{1,0:T(4,128)S(1)} %bitcast.7, f32[30,128]{1,0:T(8,128)S(1)} %get-tuple-element.10.gate_ref, bf16[32,3,80,128]{3,2,1,0:T(8,128)(2,1)S(1)} %all-to-all-done.query_ref.refs_0_, bf16[32,3,80,128]{3,2,1,0:T(8,128)(2,1)S(1)} %all-to-all-done.query_ref.refs_0_), custom_call_target="tpu_custom_call" | custom-call | flops 7864320000 | bytes 3000000 | tf_op jit(solution)/shard_map/pallas_call | solution.py:250
  94.3 0.0 all-to-all-done.3.extra_ref
  94.3 29.2 %all_to_all.20.own_ref = bf16[32,80,128]{2,1,0:T(8,128)(2,1)S(1)} all-to-all(bf16[32,80,128]{2,1,0:T(8,128)(2,1)S(1)} %shard_map.84), channel_id=1, replica_groups=mesh['x'=4,'v'=16,'y'=8] {'x','y'}, dimensions={0} | all-to-all | bytes 1310720 | tf_op jit(solution)/shard_map/all_to_all | solution.py:324
  123.5 1.1 shard_map.86
  (1 shorter events, 0.0 us)
Async XLA Ops:
  2.7 19.6 %all-to-all-start.2 = ((bf16[8,3,80,128]{3,2,1,0:T(8,128)(2,1)}), bf16[8,3,80,128]{3,2,1,0:T(8,128)(2,1)S(1)}, u32[]{:S(2)}, u32[]{:S(2)}) async-start(bf16[8,3,80,128]{3,2,1,0:T(8,128)(2,1)} %get-tuple-element.8), calls=%async_computation.2 | async-start | bytes 983040 | tf_op jit(solution)/shard_map/all_to_all | solution.py:299
  12.8 54.6 %copy-start = (s32[16,4]{0,1:T(4,128)S(1)}, s32[16,4]{0,1:T(4,128)}, u32[]{:S(2)}) copy-start(s32[16,4]{0,1:T(4,128)} %param.14) | copy-start | bytes 772
  12.8 54.6 %copy-start.1 = (s32[16,4]{0,1:T(4,128)S(1)}, s32[16,4]{0,1:T(4,128)}, u32[]{:S(2)}) copy-start(s32[16,4]{0,1:T(4,128)} %param.15) | copy-start | bytes 772
  22.3 55.7 %all-to-all-start = ((bf16[32,3,80,128]{3,2,1,0:T(8,128)(2,1)}), bf16[32,3,80,128]{3,2,1,0:T(8,128)(2,1)S(1)}, u32[]{:S(2)}, u32[]{:S(2)}) async-start(bf16[32,3,80,128]{3,2,1,0:T(8,128)(2,1)} %shard_map.83), calls=%async_computation | async-start | bytes 3932160 | tf_op jit(solution)/shard_map/all_to_all | solution.py:300
  31.1 17.8 %collective-permute-start.2 = (bf16[8,2,80,128]{3,2,1,0:T(8,128)(2,1)S(1)}, bf16[8,2,80,128]{3,2,1,0:T(8,128)(2,1)S(1)}, u32[]{:S(2)}, u32[]{:S(2)}) collective-permute-start(bf16[8,2,80,128]{3,2,1,0:T(8,128)(2,1)S(1)} %slice.4.refs_0_), channel_id=1, source_target_pairs={{0,384},{128,0},{256,128},{384,256},{1,385},{129,1},{257,129},{385... | collective-permute-start | bytes 983048 | tf_op jit(solution)/shard_map/ppermute | solution.py:294
  35.5 15.6 %collective-permute-start.1 = (bf16[8,2,80,128]{3,2,1,0:T(8,128)(2,1)S(1)}, bf16[8,2,80,128]{3,2,1,0:T(8,128)(2,1)S(1)}, u32[]{:S(2)}, u32[]{:S(2)}) collective-permute-start(bf16[8,2,80,128]{3,2,1,0:T(8,128)(2,1)S(1)} %slice.4.refs_0_), channel_id=1, source_target_pairs={{0,256},{128,384},{256,0},{384,128},{1,257},{129,385},{257,1},{385... | collective-permute-start | bytes 983048 | tf_op jit(solution)/shard_map/ppermute | solution.py:294
  37.9 29.4 %collective-permute-start = (bf16[8,2,80,128]{3,2,1,0:T(8,128)(2,1)S(1)}, bf16[8,2,80,128]{3,2,1,0:T(8,128)(2,1)}, u32[]{:S(2)}, u32[]{:S(2)}) collective-permute-start(bf16[8,2,80,128]{3,2,1,0:T(8,128)(2,1)S(1)} %slice.4.refs_0_), channel_id=1, source_target_pairs={{0,128},{128,256},{256,384},{384,0},{1,129},{129,257},{257,385},{3... | collective-permute-start | bytes 983048 | tf_op jit(solution)/shard_map/ppermute | solution.py:294
  78.0 16.3 %all-to-all-start.3 = ((bf16[8,80,128]{2,1,0:T(8,128)(2,1)}), bf16[8,80,128]{2,1,0:T(8,128)(2,1)S(1)}, u32[]{:S(2)}, u32[]{:S(2)}) async-start(bf16[8,80,128]{2,1,0:T(8,128)(2,1)} %shard_map.85), calls=%async_computation.3 | async-start | bytes 327680 | tf_op jit(solution)/shard_map/all_to_all | solution.py:315

commit v2 on v1

--- a/solution.py
+++ b/solution.py
@@ -13,13 +13,15 @@
 GROUP = 4
 CLIPS = 4
 PLANE = 32
+LONGEST_CLIP = 960
+STARTS = {2: (0,), 8: (0, 2, 4)}
 EXTRA = 8
 
 epsilon = 1e-06
 very_negative = -1e30
 exponent_scale = math.log2(math.e) / math.sqrt(HD)
 
-VMEM_BYTES = 24 * 1024 * 1024
+VMEM_BYTES = 32 * 1024 * 1024
 LARGE_VMEM = 56 * 1024 * 1024
 SMALL_VMEM = 12 * 1024 * 1024
 
@@ -142,10 +144,10 @@
 def attention_kernel(
     lengths_ref, levels_ref, gate_ref, query_ref, *refs, piece_count, first_of, places, chunk
 ):
-    piece_refs, (out_ref, key_ref, value_ref, score_ref) = refs[:piece_count], refs[piece_count:]
+    piece_refs, (out_ref, key_ref, value_ref, *score_refs) = refs[:piece_count], refs[piece_count:]
     query_place, key_place, value_place = places
     blocks, _, block_rows, _ = query_ref.shape
-    rows, _ = score_ref.shape
+    rows, _ = score_refs[0].shape
     tile_blocks, chunk_blocks = rows // block_rows, chunk // block_rows
     tiles = blocks // tile_blocks
     ends, levels = clip_table(lengths_ref, levels_ref)
@@ -171,12 +173,6 @@
     def first_row(tile):
         return first_of() + tile * rows
 
-    def last_clip(tile):
-        return clip_of(first_row(tile) + rows - 1, ends)
-
-    def chunk_count(tile):
-        return (pick(last_clip(tile), ends) + chunk - 1) // chunk
-
     def clips_of_rows(tile):
         return clip_of(first_row(tile) + lax.broadcasted_iota(jnp.int32, (rows, HD), 0), ends)
 
@@ -187,29 +183,36 @@
         held = query_ref[blocks_of(tile), query_place].reshape(rows, HD)
         return jnp.concatenate([held, clip_columns(clips_of_rows(tile))], axis=1)
 
-    def whole(tile, count):
-        extended = queries_of(tile)
-        peak = jnp.full((rows, HD), very_negative, jnp.float32)
-        for step in range(count):
-            here = slice(step * chunk, (step + 1) * chunk)
-            scores = jnp.dot(extended, key_ref[:, here], preferred_element_type=jnp.float32)
-            score_ref[:, here] = scores
-            for part in range(chunk // HD):
-                peak = jnp.maximum(peak, scores[:, part * HD : (part + 1) * HD])
-        peak = jnp.max(peak, axis=1, keepdims=True) * exponent_scale
-        peak = jnp.broadcast_to(peak, (rows, HD))
-        total = jnp.zeros((rows, HD), jnp.float32)
-        weighted = jnp.zeros((rows, HD), jnp.float32)
-        for step in range(count):
-            rounded = []
-            for part in range(chunk // HD):
-                start = step * chunk + part * HD
-                weights = jnp.exp2(score_ref[:, start : start + HD] * exponent_scale - peak)
-                total = total + weights
-                rounded.append(weights.astype(jnp.bfloat16))
-            weighted = weighted + jnp.dot(
-                jnp.concatenate(rounded, axis=1), values_of(step), preferred_element_type=jnp.float32
-            )
+    def bound(tile):
+        farthest = length if piece_count > 1 else (tile + 1) * rows + LONGEST_CLIP - 1
+        return min(length // chunk, -(-farthest // chunk))
+
+    gates = [jnp.where(level > 0, gate_ref[pl.ds(level, 1), :], 0.0) for level in levels]
+    peaks = {}
+
+    def score(tile, step, extended):
+        here = slice(step * chunk, (step + 1) * chunk)
+        scores = jnp.dot(extended, key_ref[:, here], preferred_element_type=jnp.float32)
+        score_refs[tile % 2][:, here] = scores
+        for part in range(chunk // HD):
+            peaks[tile] = jnp.maximum(peaks[tile], scores[:, part * HD : (part + 1) * HD])
+
+    def open_tile(tile):
+        peaks[tile] = jnp.full((rows, HD), very_negative, jnp.float32)
+        return queries_of(tile)
+
+    def weigh(tile, step, peak, total, weighted):
+        rounded = []
+        for part in range(chunk // HD):
+            start = step * chunk + part * HD
+            scores = score_refs[tile % 2][:, start : start + HD]
+            weights = jnp.exp2(scores * exponent_scale - peak)
+            total = total + weights
+            rounded.append(weights.astype(jnp.bfloat16))
+        rounded = jnp.concatenate(rounded, axis=1)
+        return total, weighted + jnp.dot(rounded, values_of(step), preferred_element_type=jnp.float32)
+
+    def finish(tile, total, weighted):
         attention = weighted / jnp.sum(total, axis=1, keepdims=True)
         attention = attention.astype(jnp.bfloat16).astype(jnp.float32)
         positions = first_row(tile) + lax.broadcasted_iota(jnp.int32, (rows, HD), 0)
@@ -219,25 +222,40 @@
         gated = (gate * attention).astype(jnp.bfloat16)
         out_ref[blocks_of(tile)] = gated.reshape(tile_blocks, block_rows, HD)
 
-    gates = [
-        jnp.where(level > 0, gate_ref[pl.ds(level, 1), :], 0.0) for level in levels
-    ]
-    skipped = 0
-    for tile in range(tiles):
-        skipped = skipped + (pick(last_clip(tile), levels) <= 0).astype(jnp.int32)
-
-    def clear(tile, _):
-        out_ref[blocks_of(tile)] = jnp.zeros((tile_blocks, block_rows, HD), jnp.bfloat16)
-        return 0
-
-    def one(tile, _):
-        needed = chunk_count(tile)
-        for count in range(1, length // chunk + 1):
-            pl.when(needed == count)(functools.partial(whole, tile, count))
-        return 0
-
-    lax.fori_loop(0, skipped, clear, 0)
-    lax.fori_loop(skipped, tiles, one, 0)
+    def run(first, beyond):
+        extended = open_tile(first)
+        for step in range(bound(first)):
+            score(first, step, extended)
+        for tile in range(first, beyond):
+            peak = jnp.max(peaks[tile], axis=1, keepdims=True) * exponent_scale
+            peak = jnp.broadcast_to(peak, (rows, HD))
+            total = jnp.zeros((rows, HD), jnp.float32)
+            weighted = jnp.zeros((rows, HD), jnp.float32)
+            later = bound(tile + 1) if tile + 1 < beyond else 0
+            if later:
+                extended = open_tile(tile + 1)
+            for step in range(max(bound(tile), later)):
+                if step < later:
+                    score(tile + 1, step, extended)
+                if step < bound(tile):
+                    total, weighted = weigh(tile, step, peak, total, weighted)
+            finish(tile, total, weighted)
+
+    def clear(first, beyond):
+        where = slice(first * tile_blocks, beyond * tile_blocks)
+        out_ref[where] = jnp.zeros(((beyond - first) * tile_blocks, block_rows, HD), jnp.bfloat16)
+
+    def dead(beyond):
+        return pick(clip_of(first_row(beyond) - 1, ends), levels) <= 0
+
+    for first in STARTS[tiles]:
+        begins = jnp.logical_not(dead(first + 2))
+        if first > 0:
+            begins = dead(first) if first == STARTS[tiles][-1] else jnp.logical_and(begins, dead(first))
+            pl.when(dead(first))(functools.partial(clear, first - 2, first))
+        elif tiles == 2:
+            pl.when(dead(2))(functools.partial(clear, 0, 2))
+        pl.when(begins)(functools.partial(run, first, tiles))
 
 
 def attention(
@@ -261,6 +279,7 @@
         scratch_shapes=[
             pltpu.VMEM((2 * HD, length), jnp.bfloat16),
             pltpu.VMEM((length, HD), jnp.bfloat16),
+            scores,
             scores,
         ],
         compiler_params=pltpu.CompilerParams(vmem_limit_bytes=VMEM_BYTES),

time: 125 us -> 124 us (level)
  the two profiles are of different devices: /device:TPU:73 before, /device:TPU:9 now
where the time goes in v2:
time: 124 us; the launch traced here: 123 us
  waiting for transfers between devices  40.5 us (33%)
  starting transfers between devices  30.1 us (24%)
  blocking collectives  28.8 us (23%)
  Pallas kernels  22.4 us (18%)
    all_to_all x1, blocking collectives, local(): own_back = lax.all_to_all(own_out, ('x', 'y'), 0, 0, tiled=True)  28.8 us
    ppermute x3, waiting for transfers between devices, along_x(): return lax.ppermute(value, 'x', pairs)  26.2 us
    pallas_call x2, Pallas kernels, attention(): pl.pallas_call(functools.partial(attention_kernel, piece_count=len(pieces...  15.5 us
    all_to_all x1, starting transfers between devices, local(): own_held = lax.all_to_all(own, ('x', 'y'), 0, 0, tiled=True)  9.86 us
    ppermute x3, starting transfers between devices, along_x(): return lax.ppermute(value, 'x', pairs)  9.28 us
    all_to_all x1, waiting for transfers between devices, local(): extra_held = lax.all_to_all(extra, 'y', 0, 0, tiled=True)  8.44 us
    all_to_all x1, starting transfers between devices, local(): extra_held = lax.all_to_all(extra, 'y', 0, 0, tiled=True)  6.99 us
    all_to_all x1, waiting for transfers between devices, local(): own_held = lax.all_to_all(own, ('x', 'y'), 0, 0, tiled=True)  5.88 us
  transfers between devices with their start and end apart: 6, of which 5 were waited for; matrix products, arithmetic and copies ran while one was open for 1% of the time, Pallas kernels for 15%

profile of v2, /device:TPU:9, one launch (start us, length us, event | category | flops | bytes accessed | tf_op | source)
XLA Modules:
  0.0 122.5 jit_solution(5057567292283193367)
XLA Ops:
  0.0 2.6 %shard_map.82 = (bf16[8,3,80,128]{3,2,1,0:T(8,128)(2,1)}, f32[2,80,128]{2,1,0:T(8,128)}) custom-call(bf16[80,5120]{1,0:T(8,128)(2,1)} %q_ref.3, bf16[80,5120]{1,0:T(8,128)(2,1)} %k_ref.3, bf16[80,5120]{1,0:T(8,128)(2,1)} %v_ref.3, f32[1,5120]{1,0:T(1,128)} %bitcast.8, f32[1,5120]{1,0:T(1,128)} %bitcast.10), custom_call_target="tpu_custom_call" | custom-call | flops 3000000 | bytes 3000000 | tf_op jit(solution)/shard_map/pallas_call | solution.py:83
  2.7 7.0 %all-to-all-start.2 = ((bf16[8,3,80,128]{3,2,1,0:T(8,128)(2,1)}), bf16[8,3,80,128]{3,2,1,0:T(8,128)(2,1)S(1)}, u32[]{:S(2)}, u32[]{:S(2)}) async-start(bf16[8,3,80,128]{3,2,1,0:T(8,128)(2,1)} %get-tuple-element.8), calls=%async_computation.2 | async-start | bytes 983040 | tf_op jit(solution)/shard_map/all_to_all | solution.py:318
  9.6 3.1 %shard_map.83 = bf16[32,3,80,128]{3,2,1,0:T(8,128)(2,1)} custom-call(bf16[80,5120]{1,0:T(8,128)(2,1)} %q_ref.3, bf16[80,5120]{1,0:T(8,128)(2,1)} %k_ref.3, bf16[80,5120]{1,0:T(8,128)(2,1)} %v_ref.3, f32[1,5120]{1,0:T(1,128)} %bitcast.9, f32[1,5120]{1,0:T(1,128)} %bitcast.11, f32[2,80,128]{2,1,0:T(8,128)} %get-tuple-element.7.inverse_ref), custom_call_target="tpu_custom_call" | custom-call | flops 3000000 | bytes 5000000 | tf_op jit(solution)/shard_map/pallas_call | solution.py:97
  12.8 0.0 copy-start
  12.8 0.0 copy-start.1
  12.8 8.4 %all-to-all-done.2.query_ref = bf16[8,3,80,128]{3,2,1,0:T(8,128)(2,1)S(1)} async-done(((bf16[8,3,80,128]{3,2,1,0:T(8,128)(2,1)}), bf16[8,3,80,128]{3,2,1,0:T(8,128)(2,1)S(1)}, u32[]{:S(2)}, u32[]{:S(2)}) %all-to-all-start.2) | async-done | bytes 491552 | tf_op jit(solution)/shard_map/all_to_all | solution.py:318
  21.2 9.9 %all-to-all-start = ((bf16[32,3,80,128]{3,2,1,0:T(8,128)(2,1)}), bf16[32,3,80,128]{3,2,1,0:T(8,128)(2,1)S(1)}, u32[]{:S(2)}, u32[]{:S(2)}) async-start(bf16[32,3,80,128]{3,2,1,0:T(8,128)(2,1)} %shard_map.83), calls=%async_computation | async-start | bytes 3932160 | tf_op jit(solution)/shard_map/all_to_all | solution.py:319
  31.1 4.4 %collective-permute-start.2 = (bf16[8,2,80,128]{3,2,1,0:T(8,128)(2,1)S(1)}, bf16[8,2,80,128]{3,2,1,0:T(8,128)(2,1)S(1)}, u32[]{:S(2)}, u32[]{:S(2)}) collective-permute-start(bf16[8,2,80,128]{3,2,1,0:T(8,128)(2,1)S(1)} %slice.4.refs_0_), channel_id=1, source_target_pairs={{0,384},{128,0},{256,128},{384,256},{1,385},{129,1},{257,129},{385... | collective-permute-start | bytes 983048 | tf_op jit(solution)/shard_map/ppermute | solution.py:313
  35.5 2.4 %collective-permute-start.1 = (bf16[8,2,80,128]{3,2,1,0:T(8,128)(2,1)S(1)}, bf16[8,2,80,128]{3,2,1,0:T(8,128)(2,1)S(1)}, u32[]{:S(2)}, u32[]{:S(2)}) collective-permute-start(bf16[8,2,80,128]{3,2,1,0:T(8,128)(2,1)S(1)} %slice.4.refs_0_), channel_id=1, source_target_pairs={{0,256},{128,384},{256,0},{384,128},{1,257},{129,385},{257,1},{385... | collective-permute-start | bytes 983048 | tf_op jit(solution)/shard_map/ppermute | solution.py:313
  37.9 2.5 %collective-permute-start = (bf16[8,2,80,128]{3,2,1,0:T(8,128)(2,1)S(1)}, bf16[8,2,80,128]{3,2,1,0:T(8,128)(2,1)}, u32[]{:S(2)}, u32[]{:S(2)}) collective-permute-start(bf16[8,2,80,128]{3,2,1,0:T(8,128)(2,1)S(1)} %slice.4.refs_0_), channel_id=1, source_target_pairs={{0,128},{128,256},{256,384},{384,0},{1,129},{129,257},{257,385},{3... | collective-permute-start | bytes 983048 | tf_op jit(solution)/shard_map/ppermute | solution.py:313
  40.4 0.7 constant_dynamic-slice_fusion
  41.2 7.7 %collective-permute-done.2.refs_3_ = bf16[8,2,80,128]{3,2,1,0:T(8,128)(2,1)S(1)} collective-permute-done((bf16[8,2,80,128]{3,2,1,0:T(8,128)(2,1)S(1)}, bf16[8,2,80,128]{3,2,1,0:T(8,128)(2,1)S(1)}, u32[]{:S(2)}, u32[]{:S(2)}) %collective-permute-start.2) | collective-permute-done | bytes 327712 | tf_op jit(solution)/shard_map/ppermute | solution.py:313
  48.9 2.2 %collective-permute-done.1.refs_2_ = bf16[8,2,80,128]{3,2,1,0:T(8,128)(2,1)S(1)} collective-permute-done((bf16[8,2,80,128]{3,2,1,0:T(8,128)(2,1)S(1)}, bf16[8,2,80,128]{3,2,1,0:T(8,128)(2,1)S(1)}, u32[]{:S(2)}, u32[]{:S(2)}) %collective-permute-start.1) | collective-permute-done | bytes 327712 | tf_op jit(solution)/shard_map/ppermute | solution.py:313
  51.1 16.3 %collective-permute-done.refs_1_ = bf16[8,2,80,128]{3,2,1,0:T(8,128)(2,1)} collective-permute-done((bf16[8,2,80,128]{3,2,1,0:T(8,128)(2,1)S(1)}, bf16[8,2,80,128]{3,2,1,0:T(8,128)(2,1)}, u32[]{:S(2)}, u32[]{:S(2)}) %collective-permute-start) | collective-permute-done | bytes 327712 | tf_op jit(solution)/shard_map/ppermute | solution.py:313
  67.3 0.0 copy-done
  67.3 0.0 copy-done.1
  67.3 4.8 %shard_map.85 = bf16[8,80,128]{2,1,0:T(8,128)(2,1)} custom-call(s32[4,16]{1,0:T(4,128)S(1)} %bitcast.4, s32[4,16]{1,0:T(4,128)S(1)} %bitcast.6, f32[30,128]{1,0:T(8,128)S(1)} %get-tuple-element.9.gate_ref, bf16[8,3,80,128]{3,2,1,0:T(8,128)(2,1)S(1)} %all-to-all-done.2.query_ref, bf16[8,2,80,128]{3,2,1,0:T(8,128)(2,1)S(1)} %slice.4.refs_0_, ...), custom_call_target="tpu_custom_call" | custom-call | flops 1966080000 | bytes 3000000 | tf_op jit(solution)/shard_map/pallas_call | solution.py:268
  72.1 5.9 %all-to-all-done.query_ref.refs_0_ = bf16[32,3,80,128]{3,2,1,0:T(8,128)(2,1)S(1)} async-done(((bf16[32,3,80,128]{3,2,1,0:T(8,128)(2,1)}), bf16[32,3,80,128]{3,2,1,0:T(8,128)(2,1)S(1)}, u32[]{:S(2)}, u32[]{:S(2)}) %all-to-all-start) | async-done | bytes 1966112 | tf_op jit(solution)/shard_map/all_to_all | solution.py:319
  78.0 3.9 %all-to-all-start.3 = ((bf16[8,80,128]{2,1,0:T(8,128)(2,1)}), bf16[8,80,128]{2,1,0:T(8,128)(2,1)S(1)}, u32[]{:S(2)}, u32[]{:S(2)}) async-start(bf16[8,80,128]{2,1,0:T(8,128)(2,1)} %shard_map.85), calls=%async_computation.3 | async-start | bytes 327680 | tf_op jit(solution)/shard_map/all_to_all | solution.py:334
  81.9 10.8 %shard_map.84 = bf16[32,80,128]{2,1,0:T(8,128)(2,1)S(1)} custom-call(s32[4,16]{1,0:T(4,128)S(1)} %bitcast.5, s32[4,16]{1,0:T(4,128)S(1)} %bitcast.7, f32[30,128]{1,0:T(8,128)S(1)} %get-tuple-element.10.gate_ref, bf16[32,3,80,128]{3,2,1,0:T(8,128)(2,1)S(1)} %all-to-all-done.query_ref.refs_0_, bf16[32,3,80,128]{3,2,1,0:T(8,128)(2,1)S(1)} %all-to-all-done.query_ref.refs_0_), custom_call_target="tpu_custom_call" | custom-call | flops 7864320000 | bytes 3000000 | tf_op jit(solution)/shard_map/pallas_call | solution.py:268
  92.7 0.0 all-to-all-done.3.extra_ref
  92.7 28.8 %all_to_all.20.own_ref = bf16[32,80,128]{2,1,0:T(8,128)(2,1)S(1)} all-to-all(bf16[32,80,128]{2,1,0:T(8,128)(2,1)S(1)} %shard_map.84), channel_id=1, replica_groups=mesh['x'=4,'v'=16,'y'=8] {'x','y'}, dimensions={0} | all-to-all | bytes 1310720 | tf_op jit(solution)/shard_map/all_to_all | solution.py:343
  121.5 1.1 shard_map.86
  (1 shorter events, 0.0 us)
Async XLA Ops:
  2.7 18.6 %all-to-all-start.2 = ((bf16[8,3,80,128]{3,2,1,0:T(8,128)(2,1)}), bf16[8,3,80,128]{3,2,1,0:T(8,128)(2,1)S(1)}, u32[]{:S(2)}, u32[]{:S(2)}) async-start(bf16[8,3,80,128]{3,2,1,0:T(8,128)(2,1)} %get-tuple-element.8), calls=%async_computation.2 | async-start | bytes 983040 | tf_op jit(solution)/shard_map/all_to_all | solution.py:318
  12.8 54.6 %copy-start = (s32[16,4]{0,1:T(4,128)S(1)}, s32[16,4]{0,1:T(4,128)}, u32[]{:S(2)}) copy-start(s32[16,4]{0,1:T(4,128)} %param.14) | copy-start | bytes 772
  12.8 54.6 %copy-start.1 = (s32[16,4]{0,1:T(4,128)S(1)}, s32[16,4]{0,1:T(4,128)}, u32[]{:S(2)}) copy-start(s32[16,4]{0,1:T(4,128)} %param.15) | copy-start | bytes 772
  21.2 56.8 %all-to-all-start = ((bf16[32,3,80,128]{3,2,1,0:T(8,128)(2,1)}), bf16[32,3,80,128]{3,2,1,0:T(8,128)(2,1)S(1)}, u32[]{:S(2)}, u32[]{:S(2)}) async-start(bf16[32,3,80,128]{3,2,1,0:T(8,128)(2,1)} %shard_map.83), calls=%async_computation | async-start | bytes 3932160 | tf_op jit(solution)/shard_map/all_to_all | solution.py:319
  31.1 17.8 %collective-permute-start.2 = (bf16[8,2,80,128]{3,2,1,0:T(8,128)(2,1)S(1)}, bf16[8,2,80,128]{3,2,1,0:T(8,128)(2,1)S(1)}, u32[]{:S(2)}, u32[]{:S(2)}) collective-permute-start(bf16[8,2,80,128]{3,2,1,0:T(8,128)(2,1)S(1)} %slice.4.refs_0_), channel_id=1, source_target_pairs={{0,384},{128,0},{256,128},{384,256},{1,385},{129,1},{257,129},{385... | collective-permute-start | bytes 983048 | tf_op jit(solution)/shard_map/ppermute | solution.py:313
  35.5 15.6 %collective-permute-start.1 = (bf16[8,2,80,128]{3,2,1,0:T(8,128)(2,1)S(1)}, bf16[8,2,80,128]{3,2,1,0:T(8,128)(2,1)S(1)}, u32[]{:S(2)}, u32[]{:S(2)}) collective-permute-start(bf16[8,2,80,128]{3,2,1,0:T(8,128)(2,1)S(1)} %slice.4.refs_0_), channel_id=1, source_target_pairs={{0,256},{128,384},{256,0},{384,128},{1,257},{129,385},{257,1},{385... | collective-permute-start | bytes 983048 | tf_op jit(solution)/shard_map/ppermute | solution.py:313
  37.9 29.4 %collective-permute-start = (bf16[8,2,80,128]{3,2,1,0:T(8,128)(2,1)S(1)}, bf16[8,2,80,128]{3,2,1,0:T(8,128)(2,1)}, u32[]{:S(2)}, u32[]{:S(2)}) collective-permute-start(bf16[8,2,80,128]{3,2,1,0:T(8,128)(2,1)S(1)} %slice.4.refs_0_), channel_id=1, source_target_pairs={{0,128},{128,256},{256,384},{384,0},{1,129},{129,257},{257,385},{3... | collective-permute-start | bytes 983048 | tf_op jit(solution)/shard_map/ppermute | solution.py:313
  78.0 14.7 %all-to-all-start.3 = ((bf16[8,80,128]{2,1,0:T(8,128)(2,1)}), bf16[8,80,128]{2,1,0:T(8,128)(2,1)S(1)}, u32[]{:S(2)}, u32[]{:S(2)}) async-start(bf16[8,80,128]{2,1,0:T(8,128)(2,1)} %shard_map.85), calls=%async_computation.3 | async-start | bytes 327680 | tf_op jit(solution)/shard_map/all_to_all | solution.py:334

commit v3 on v2

--- a/solution.py
+++ b/solution.py
@@ -144,7 +144,7 @@
 def attention_kernel(
     lengths_ref, levels_ref, gate_ref, query_ref, *refs, piece_count, first_of, places, chunk
 ):
-    piece_refs, (out_ref, key_ref, value_ref, *score_refs) = refs[:piece_count], refs[piece_count:]
+    piece_refs, (out_ref, key_ref, *score_refs) = refs[:piece_count], refs[piece_count:]
     query_place, key_place, value_place = places
     blocks, _, block_rows, _ = query_ref.shape
     rows, _ = score_refs[0].shape
@@ -152,23 +152,23 @@
     tiles = blocks // tile_blocks
     ends, levels = clip_table(lengths_ref, levels_ref)
 
-    length, piece_rows = key_ref.shape[1], key_ref.shape[1] // piece_count
-    for turn, piece_ref in enumerate(piece_refs):
-        place = (lax.axis_index("x") + GROUP - turn) % GROUP if piece_count > 1 else 0
-        for step in range(piece_rows // chunk):
-            start = place * piece_rows + step * chunk
-            where = pl.ds(pl.multiple_of(start, chunk), chunk)
-            source = slice(step * chunk_blocks, (step + 1) * chunk_blocks)
-            key_ref[0:HD, where] = piece_ref[source, key_place].reshape(chunk, HD).T
-            key_ref[HD : HD + 16, where] = blocked_rows(start, chunk, ends)
-            if piece_count > 1:
-                value_ref[where, :] = piece_ref[source, value_place].reshape(chunk, HD)
-    key_ref[HD + 16 :, :] = jnp.zeros((HD - 16, length), jnp.bfloat16)
+    length = key_ref.shape[1]
+    piece_chunks = length // chunk // piece_count
+
+    def fill(step):
+        turn, part = step // piece_chunks, step % piece_chunks
+        source = slice(part * chunk_blocks, (part + 1) * chunk_blocks)
+        where = slice(step * chunk, (step + 1) * chunk)
+        place = (lax.axis_index("x") + GROUP - turn) % GROUP if piece_count > 1 else turn
+        start = (place * piece_chunks + part) * chunk
+        key_ref[0:HD, where] = piece_refs[turn][source, key_place].reshape(chunk, HD).T
+        key_ref[HD : HD + 16, where] = blocked_rows(start, chunk, ends)
+        key_ref[HD + 16 :, where] = jnp.zeros((HD - 16, chunk), jnp.bfloat16)
 
     def values_of(step):
-        if piece_count > 1:
-            return value_ref[step * chunk : (step + 1) * chunk, :]
-        return piece_refs[0][step * chunk_blocks : (step + 1) * chunk_blocks, value_place].reshape(chunk, HD)
+        turn, part = step // piece_chunks, step % piece_chunks
+        source = slice(part * chunk_blocks, (part + 1) * chunk_blocks)
+        return piece_refs[turn][source, value_place].reshape(chunk, HD)
 
     def first_row(tile):
         return first_of() + tile * rows
@@ -190,7 +190,10 @@
     gates = [jnp.where(level > 0, gate_ref[pl.ds(level, 1), :], 0.0) for level in levels]
     peaks = {}
 
-    def score(tile, step, extended):
+    def score(tile, step, extended, filled):
+        if step not in filled:
+            fill(step)
+            filled.append(step)
         here = slice(step * chunk, (step + 1) * chunk)
         scores = jnp.dot(extended, key_ref[:, here], preferred_element_type=jnp.float32)
         score_refs[tile % 2][:, here] = scores
@@ -223,9 +226,10 @@
         out_ref[blocks_of(tile)] = gated.reshape(tile_blocks, block_rows, HD)
 
     def run(first, beyond):
+        filled = []
         extended = open_tile(first)
         for step in range(bound(first)):
-            score(first, step, extended)
+            score(first, step, extended, filled)
         for tile in range(first, beyond):
             peak = jnp.max(peaks[tile], axis=1, keepdims=True) * exponent_scale
             peak = jnp.broadcast_to(peak, (rows, HD))
@@ -236,7 +240,7 @@
                 extended = open_tile(tile + 1)
             for step in range(max(bound(tile), later)):
                 if step < later:
-                    score(tile + 1, step, extended)
+                    score(tile + 1, step, extended, filled)
                 if step < bound(tile):
                     total, weighted = weigh(tile, step, peak, total, weighted)
             finish(tile, total, weighted)
@@ -278,7 +282,6 @@
         out_specs=vmem(),
         scratch_shapes=[
             pltpu.VMEM((2 * HD, length), jnp.bfloat16),
-            pltpu.VMEM((length, HD), jnp.bfloat16),
             scores,
             scores,
         ],

time: 124 us -> 124 us (level)
  no operation moved by 1% of the time
where the time goes in v3:
time: 124 us; the launch traced here: 122 us
  waiting for transfers between devices  40.7 us (33%)
  starting transfers between devices  30.1 us (24%)
  blocking collectives  27.9 us (22%)
  Pallas kernels  22.2 us (18%)
    all_to_all x1, blocking collectives, local(): own_back = lax.all_to_all(own_out, ('x', 'y'), 0, 0, tiled=True)  27.9 us
    ppermute x3, waiting for transfers between devices, along_x(): return lax.ppermute(value, 'x', pairs)  26.2 us
    pallas_call x2, Pallas kernels, attention(): pl.pallas_call(functools.partial(attention_kernel, piece_count=len(pieces...  15.3 us
    all_to_all x1, starting transfers between devices, local(): own_held = lax.all_to_all(own, ('x', 'y'), 0, 0, tiled=True)  9.86 us
    ppermute x3, starting transfers between devices, along_x(): return lax.ppermute(value, 'x', pairs)  9.28 us
    all_to_all x1, waiting for transfers between devices, local(): extra_held = lax.all_to_all(extra, 'y', 0, 0, tiled=True)  8.44 us
    all_to_all x1, starting transfers between devices, local(): extra_held = lax.all_to_all(extra, 'y', 0, 0, tiled=True)  6.99 us
    all_to_all x1, waiting for transfers between devices, local(): own_held = lax.all_to_all(own, ('x', 'y'), 0, 0, tiled=True)  6.03 us
  transfers between devices with their start and end apart: 6, of which 5 were waited for; matrix products, arithmetic and copies ran while one was open for 1% of the time, Pallas kernels for 15%

profile of v3, /device:TPU:9, one launch (start us, length us, event | category | flops | bytes accessed | tf_op | source)
XLA Modules:
  0.0 121.7 jit_solution(13373164673677082728)
XLA Ops:
  0.0 2.6 %shard_map.82 = (bf16[8,3,80,128]{3,2,1,0:T(8,128)(2,1)}, f32[2,80,128]{2,1,0:T(8,128)}) custom-call(bf16[80,5120]{1,0:T(8,128)(2,1)} %q_ref.3, bf16[80,5120]{1,0:T(8,128)(2,1)} %k_ref.3, bf16[80,5120]{1,0:T(8,128)(2,1)} %v_ref.3, f32[1,5120]{1,0:T(1,128)} %bitcast.8, f32[1,5120]{1,0:T(1,128)} %bitcast.10), custom_call_target="tpu_custom_call" | custom-call | flops 3000000 | bytes 3000000 | tf_op jit(solution)/shard_map/pallas_call | solution.py:83
  2.7 7.0 %all-to-all-start.2 = ((bf16[8,3,80,128]{3,2,1,0:T(8,128)(2,1)}), bf16[8,3,80,128]{3,2,1,0:T(8,128)(2,1)S(1)}, u32[]{:S(2)}, u32[]{:S(2)}) async-start(bf16[8,3,80,128]{3,2,1,0:T(8,128)(2,1)} %get-tuple-element.8), calls=%async_computation.2 | async-start | bytes 983040 | tf_op jit(solution)/shard_map/all_to_all | solution.py:321
  9.6 3.1 %shard_map.83 = bf16[32,3,80,128]{3,2,1,0:T(8,128)(2,1)} custom-call(bf16[80,5120]{1,0:T(8,128)(2,1)} %q_ref.3, bf16[80,5120]{1,0:T(8,128)(2,1)} %k_ref.3, bf16[80,5120]{1,0:T(8,128)(2,1)} %v_ref.3, f32[1,5120]{1,0:T(1,128)} %bitcast.9, f32[1,5120]{1,0:T(1,128)} %bitcast.11, f32[2,80,128]{2,1,0:T(8,128)} %get-tuple-element.7.inverse_ref), custom_call_target="tpu_custom_call" | custom-call | flops 3000000 | bytes 5000000 | tf_op jit(solution)/shard_map/pallas_call | solution.py:97
  12.8 0.0 copy-start
  12.8 0.0 copy-start.1
  12.8 8.4 %all-to-all-done.2.query_ref = bf16[8,3,80,128]{3,2,1,0:T(8,128)(2,1)S(1)} async-done(((bf16[8,3,80,128]{3,2,1,0:T(8,128)(2,1)}), bf16[8,3,80,128]{3,2,1,0:T(8,128)(2,1)S(1)}, u32[]{:S(2)}, u32[]{:S(2)}) %all-to-all-start.2) | async-done | bytes 491552 | tf_op jit(solution)/shard_map/all_to_all | solution.py:321
  21.2 9.9 %all-to-all-start = ((bf16[32,3,80,128]{3,2,1,0:T(8,128)(2,1)}), bf16[32,3,80,128]{3,2,1,0:T(8,128)(2,1)S(1)}, u32[]{:S(2)}, u32[]{:S(2)}) async-start(bf16[32,3,80,128]{3,2,1,0:T(8,128)(2,1)} %shard_map.83), calls=%async_computation | async-start | bytes 3932160 | tf_op jit(solution)/shard_map/all_to_all | solution.py:322
  31.1 4.4 %collective-permute-start.2 = (bf16[8,2,80,128]{3,2,1,0:T(8,128)(2,1)S(1)}, bf16[8,2,80,128]{3,2,1,0:T(8,128)(2,1)S(1)}, u32[]{:S(2)}, u32[]{:S(2)}) collective-permute-start(bf16[8,2,80,128]{3,2,1,0:T(8,128)(2,1)S(1)} %slice.4.refs_0_), channel_id=1, source_target_pairs={{0,384},{128,0},{256,128},{384,256},{1,385},{129,1},{257,129},{385... | collective-permute-start | bytes 983048 | tf_op jit(solution)/shard_map/ppermute | solution.py:316
  35.5 2.4 %collective-permute-start.1 = (bf16[8,2,80,128]{3,2,1,0:T(8,128)(2,1)S(1)}, bf16[8,2,80,128]{3,2,1,0:T(8,128)(2,1)S(1)}, u32[]{:S(2)}, u32[]{:S(2)}) collective-permute-start(bf16[8,2,80,128]{3,2,1,0:T(8,128)(2,1)S(1)} %slice.4.refs_0_), channel_id=1, source_target_pairs={{0,256},{128,384},{256,0},{384,128},{1,257},{129,385},{257,1},{385... | collective-permute-start | bytes 983048 | tf_op jit(solution)/shard_map/ppermute | solution.py:316
  37.9 2.5 %collective-permute-start = (bf16[8,2,80,128]{3,2,1,0:T(8,128)(2,1)S(1)}, bf16[8,2,80,128]{3,2,1,0:T(8,128)(2,1)}, u32[]{:S(2)}, u32[]{:S(2)}) collective-permute-start(bf16[8,2,80,128]{3,2,1,0:T(8,128)(2,1)S(1)} %slice.4.refs_0_), channel_id=1, source_target_pairs={{0,128},{128,256},{256,384},{384,0},{1,129},{129,257},{257,385},{3... | collective-permute-start | bytes 983048 | tf_op jit(solution)/shard_map/ppermute | solution.py:316
  40.4 0.7 constant_dynamic-slice_fusion
  41.2 7.7 %collective-permute-done.2.refs_3_ = bf16[8,2,80,128]{3,2,1,0:T(8,128)(2,1)S(1)} collective-permute-done((bf16[8,2,80,128]{3,2,1,0:T(8,128)(2,1)S(1)}, bf16[8,2,80,128]{3,2,1,0:T(8,128)(2,1)S(1)}, u32[]{:S(2)}, u32[]{:S(2)}) %collective-permute-start.2) | collective-permute-done | bytes 327712 | tf_op jit(solution)/shard_map/ppermute | solution.py:316
  48.9 2.2 %collective-permute-done.1.refs_2_ = bf16[8,2,80,128]{3,2,1,0:T(8,128)(2,1)S(1)} collective-permute-done((bf16[8,2,80,128]{3,2,1,0:T(8,128)(2,1)S(1)}, bf16[8,2,80,128]{3,2,1,0:T(8,128)(2,1)S(1)}, u32[]{:S(2)}, u32[]{:S(2)}) %collective-permute-start.1) | collective-permute-done | bytes 327712 | tf_op jit(solution)/shard_map/ppermute | solution.py:316
  51.1 16.3 %collective-permute-done.refs_1_ = bf16[8,2,80,128]{3,2,1,0:T(8,128)(2,1)} collective-permute-done((bf16[8,2,80,128]{3,2,1,0:T(8,128)(2,1)S(1)}, bf16[8,2,80,128]{3,2,1,0:T(8,128)(2,1)}, u32[]{:S(2)}, u32[]{:S(2)}) %collective-permute-start) | collective-permute-done | bytes 327712 | tf_op jit(solution)/shard_map/ppermute | solution.py:316
  67.3 0.0 copy-done
  67.3 0.0 copy-done.1
  67.3 4.6 %shard_map.85 = bf16[8,80,128]{2,1,0:T(8,128)(2,1)} custom-call(s32[4,16]{1,0:T(4,128)S(1)} %bitcast.4, s32[4,16]{1,0:T(4,128)S(1)} %bitcast.6, f32[30,128]{1,0:T(8,128)S(1)} %get-tuple-element.9.gate_ref, bf16[8,3,80,128]{3,2,1,0:T(8,128)(2,1)S(1)} %all-to-all-done.2.query_ref, bf16[8,2,80,128]{3,2,1,0:T(8,128)(2,1)S(1)} %slice.4.refs_0_, ...), custom_call_target="tpu_custom_call" | custom-call | flops 1966080000 | bytes 3000000 | tf_op jit(solution)/shard_map/pallas_call | solution.py:272
  72.0 6.0 %all-to-all-done.query_ref.refs_0_ = bf16[32,3,80,128]{3,2,1,0:T(8,128)(2,1)S(1)} async-done(((bf16[32,3,80,128]{3,2,1,0:T(8,128)(2,1)}), bf16[32,3,80,128]{3,2,1,0:T(8,128)(2,1)S(1)}, u32[]{:S(2)}, u32[]{:S(2)}) %all-to-all-start) | async-done | bytes 1966112 | tf_op jit(solution)/shard_map/all_to_all | solution.py:322
  78.0 3.9 %all-to-all-start.3 = ((bf16[8,80,128]{2,1,0:T(8,128)(2,1)}), bf16[8,80,128]{2,1,0:T(8,128)(2,1)S(1)}, u32[]{:S(2)}, u32[]{:S(2)}) async-start(bf16[8,80,128]{2,1,0:T(8,128)(2,1)} %shard_map.85), calls=%async_computation.3 | async-start | bytes 327680 | tf_op jit(solution)/shard_map/all_to_all | solution.py:337
  81.9 10.7 %shard_map.84 = bf16[32,80,128]{2,1,0:T(8,128)(2,1)S(1)} custom-call(s32[4,16]{1,0:T(4,128)S(1)} %bitcast.5, s32[4,16]{1,0:T(4,128)S(1)} %bitcast.7, f32[30,128]{1,0:T(8,128)S(1)} %get-tuple-element.10.gate_ref, bf16[32,3,80,128]{3,2,1,0:T(8,128)(2,1)S(1)} %all-to-all-done.query_ref.refs_0_, bf16[32,3,80,128]{3,2,1,0:T(8,128)(2,1)S(1)} %all-to-all-done.query_ref.refs_0_), custom_call_target="tpu_custom_call" | custom-call | flops 7864320000 | bytes 3000000 | tf_op jit(solution)/shard_map/pallas_call | solution.py:272
  92.6 0.0 all-to-all-done.3.extra_ref
  92.7 27.9 %all_to_all.20.own_ref = bf16[32,80,128]{2,1,0:T(8,128)(2,1)S(1)} all-to-all(bf16[32,80,128]{2,1,0:T(8,128)(2,1)S(1)} %shard_map.84), channel_id=1, replica_groups=mesh['x'=4,'v'=16,'y'=8] {'x','y'}, dimensions={0} | all-to-all | bytes 1310720 | tf_op jit(solution)/shard_map/all_to_all | solution.py:346
  120.6 1.1 shard_map.86
  (1 shorter events, 0.0 us)
Async XLA Ops:
  2.7 18.6 %all-to-all-start.2 = ((bf16[8,3,80,128]{3,2,1,0:T(8,128)(2,1)}), bf16[8,3,80,128]{3,2,1,0:T(8,128)(2,1)S(1)}, u32[]{:S(2)}, u32[]{:S(2)}) async-start(bf16[8,3,80,128]{3,2,1,0:T(8,128)(2,1)} %get-tuple-element.8), calls=%async_computation.2 | async-start | bytes 983040 | tf_op jit(solution)/shard_map/all_to_all | solution.py:321
  12.8 54.6 %copy-start = (s32[16,4]{0,1:T(4,128)S(1)}, s32[16,4]{0,1:T(4,128)}, u32[]{:S(2)}) copy-start(s32[16,4]{0,1:T(4,128)} %param.14) | copy-start | bytes 772
  12.8 54.6 %copy-start.1 = (s32[16,4]{0,1:T(4,128)S(1)}, s32[16,4]{0,1:T(4,128)}, u32[]{:S(2)}) copy-start(s32[16,4]{0,1:T(4,128)} %param.15) | copy-start | bytes 772
  21.2 56.8 %all-to-all-start = ((bf16[32,3,80,128]{3,2,1,0:T(8,128)(2,1)}), bf16[32,3,80,128]{3,2,1,0:T(8,128)(2,1)S(1)}, u32[]{:S(2)}, u32[]{:S(2)}) async-start(bf16[32,3,80,128]{3,2,1,0:T(8,128)(2,1)} %shard_map.83), calls=%async_computation | async-start | bytes 3932160 | tf_op jit(solution)/shard_map/all_to_all | solution.py:322
  31.1 17.8 %collective-permute-start.2 = (bf16[8,2,80,128]{3,2,1,0:T(8,128)(2,1)S(1)}, bf16[8,2,80,128]{3,2,1,0:T(8,128)(2,1)S(1)}, u32[]{:S(2)}, u32[]{:S(2)}) collective-permute-start(bf16[8,2,80,128]{3,2,1,0:T(8,128)(2,1)S(1)} %slice.4.refs_0_), channel_id=1, source_target_pairs={{0,384},{128,0},{256,128},{384,256},{1,385},{129,1},{257,129},{385... | collective-permute-start | bytes 983048 | tf_op jit(solution)/shard_map/ppermute | solution.py:316
  35.5 15.6 %collective-permute-start.1 = (bf16[8,2,80,128]{3,2,1,0:T(8,128)(2,1)S(1)}, bf16[8,2,80,128]{3,2,1,0:T(8,128)(2,1)S(1)}, u32[]{:S(2)}, u32[]{:S(2)}) collective-permute-start(bf16[8,2,80,128]{3,2,1,0:T(8,128)(2,1)S(1)} %slice.4.refs_0_), channel_id=1, source_target_pairs={{0,256},{128,384},{256,0},{384,128},{1,257},{129,385},{257,1},{385... | collective-permute-start | bytes 983048 | tf_op jit(solution)/shard_map/ppermute | solution.py:316
  37.9 29.4 %collective-permute-start = (bf16[8,2,80,128]{3,2,1,0:T(8,128)(2,1)S(1)}, bf16[8,2,80,128]{3,2,1,0:T(8,128)(2,1)}, u32[]{:S(2)}, u32[]{:S(2)}) collective-permute-start(bf16[8,2,80,128]{3,2,1,0:T(8,128)(2,1)S(1)} %slice.4.refs_0_), channel_id=1, source_target_pairs={{0,128},{128,256},{256,384},{384,0},{1,129},{129,257},{257,385},{3... | collective-permute-start | bytes 983048 | tf_op jit(solution)/shard_map/ppermute | solution.py:316
  78.0 14.7 %all-to-all-start.3 = ((bf16[8,80,128]{2,1,0:T(8,128)(2,1)}), bf16[8,80,128]{2,1,0:T(8,128)(2,1)S(1)}, u32[]{:S(2)}, u32[]{:S(2)}) async-start(bf16[8,80,128]{2,1,0:T(8,128)(2,1)} %shard_map.85), calls=%async_computation.3 | async-start | bytes 327680 | tf_op jit(solution)/shard_map/all_to_all | solution.py:337
